TPU v7x, 32 devices: a whole 2x2x4 slice. The times are simulated.
32 devices in a mesh: ctx: 4 (over x, core), ch: 8 (over z, y).
Axes of the slice: x: 2, y: 2, z: 4, core: 2. Of those that a mesh axis runs over, the one named last changes fastest.
Arguments:
- streams: bfloat16 [3, 4608, 1024], P(None, 'ch', 'ctx'), may hold values from -6 to 6
- short_taps: float32 [3, 4608, 3], P(None, 'ch'), may hold values from -1 to 1
- filter_in: float32 [32, 64], replicated, may hold values from -1 to 1
- filter_mid: float32 [64, 64], replicated, may hold values from -0.75 to 0.75
- filter_out: float32 [64, 4608], P(None, 'ch'), may hold values from -2 to 2
- decay_rate: float32 [4608], P('ch'), as said below
- skip_gain: float32 [4608], P('ch'), may hold values from 0.5 to 1.5
- out_weight: bfloat16 [4608, 4608], P('ch'), may hold values from -0.09375 to 0.09375
- grad_out: bfloat16 [4608, 1024], P('ch', 'ctx'), may hold values from -6 to 6
Outputs:
- layer_out: bfloat16 [4608, 1024], P('ch', 'ctx')
- grad_streams: bfloat16 [3, 4608, 1024], P(None, 'ch', 'ctx')
- grad_filter_in: float32 [32, 64], replicated
- grad_filter_mid: float32 [64, 64], replicated
- grad_filter_out: float32 [64, 4608], P(None, 'ch')
- grad_out_weight: float32 [4608, 4608], P('ch')
Inputs may be any that keep to these rules, and one draw needn't show every extreme that they name: `decay_rate`: every channel's rate lies between 1 / 5120 and 1 / 30.
All inputs are finite; a program needn't handle non-finite values.
Results may differ from a plain program's by a relative error of at most 0.014.
Values may be sent and summed in bfloat16 or wider, within the bound.
A program may use at most 128 MiB of HBM per device.

v0:
```python
import functools
import math

import jax
import jax.numpy as jnp
import numpy as np
from jax import lax
from jax.experimental import pallas as pl
from jax.experimental.pallas import tpu as pltpu
from jax.sharding import PartitionSpec as P

precise = lax.Precision.HIGHEST
MESH = pl.DeviceIdType.MESH


def arrived(ref, sem):
    pltpu.make_async_copy(ref, ref, sem).wait()


def greet(friends):
    barrier = pltpu.get_barrier_semaphore()
    for friend in friends:
        pl.semaphore_signal(barrier, inc=1, device_id=friend, device_id_type=MESH)
    pl.semaphore_wait(barrier, len(friends))


def remote(src, dst, send_sem, recv_sem, target):
    copy = pltpu.make_async_remote_copy(
        src_ref=src,
        dst_ref=dst,
        send_sem=send_sem,
        recv_sem=recv_sem,
        device_id=target,
        device_id_type=MESH,
    )
    copy.start()
    return copy


def in_any(count):
    return [pl.BlockSpec(memory_space=pl.ANY)] * count


def to_sequence_kernel(cycle, tokens, in_ref, out_ref, send_sem, recv_sem, own_sem):
    me = lax.axis_index("ctx")
    peers = [lax.rem(me + step, cycle) for step in range(cycle)]
    greet([{"ctx": peer} for peer in peers[1:]])
    place = out_ref.at[:, :, pl.ds(pl.multiple_of(me * tokens, tokens), tokens)]
    copies = [
        remote(in_ref.at[:, peers[s]], place, send_sem.at[s], recv_sem.at[s], {"ctx": peers[s]})
        for s in range(1, cycle)
    ]
    own = pltpu.make_async_copy(in_ref.at[:, me], place, own_sem)
    own.start()
    own.wait()
    for copy in copies:
        copy.wait()


def to_sequence(ident, pieces):
    streams, cycle, share, tokens = pieces.shape
    return pl.pallas_call(
        functools.partial(to_sequence_kernel, cycle, tokens),
        out_shape=jax.ShapeDtypeStruct((streams, share, cycle * tokens), pieces.dtype),
        in_specs=in_any(1),
        out_specs=pl.BlockSpec(memory_space=pl.ANY),
        scratch_shapes=[
            pltpu.SemaphoreType.DMA((cycle,)),
            pltpu.SemaphoreType.DMA((cycle,)),
            pltpu.SemaphoreType.DMA,
        ],
        compiler_params=pltpu.CompilerParams(collective_id=ident, has_side_effects=True),
    )(pieces)


def finish_kernel(
    cycle, groups, tokens, seq_ref, last_ref, small_ref, out_ref, last_out, small_out,
    from_ctx, mine, from_ch, send_sem, recv_sem, own_sem, ch_send, ch_recv,
):
    me, group = lax.axis_index("ctx"), lax.axis_index("ch")
    peers = [lax.rem(me + step, cycle) for step in range(cycle)]
    others = [lax.rem(group + step, groups) for step in range(groups)]
    greet([{"ctx": p} for p in peers[1:]] + [{"ch": p} for p in others[1:]])
    small_copies, copies = [], []
    for s in range(1, cycle):
        to = {"ctx": peers[s]}
        small_copies.append(
            remote(small_ref, from_ctx.at[me], send_sem.at[0, s], recv_sem.at[0, s], to)
        )
    for s in range(1, cycle):
        to = {"ctx": peers[s]}
        src = seq_ref.at[:, :, pl.ds(pl.multiple_of(peers[s] * tokens, tokens), tokens)]
        copies.append(remote(src, out_ref.at[:, me], send_sem.at[1, s], recv_sem.at[1, s], to))
        copies.append(remote(last_ref, last_out.at[me], send_sem.at[2, s], recv_sem.at[2, s], to))
    src = seq_ref.at[:, :, pl.ds(pl.multiple_of(me * tokens, tokens), tokens)]
    owns = [
        pltpu.make_async_copy(src, out_ref.at[:, me], own_sem.at[0]),
        pltpu.make_async_copy(last_ref, last_out.at[me], own_sem.at[1]),
    ]
    for own in owns:
        own.start()
    from_ctx[me] = small_ref[...]
    for copy in small_copies:
        copy.wait()
    mine[...] = total(from_ctx[j] for j in range(cycle))
    small_copies = [
        remote(mine, from_ch.at[group], ch_send.at[s], ch_recv.at[s], {"ch": others[s]})
        for s in range(1, groups)
    ]
    from_ch[group] = mine[...]
    for copy in small_copies:
        copy.wait()
    small_out[...] = total(from_ch[i] for i in range(groups))
    for copy in owns + copies:
        copy.wait()


def finish(ident, seq, last, small, tokens):
    cycle, groups = lax.axis_size("ctx"), lax.axis_size("ch")
    streams, share, _ = seq.shape
    vmem = pl.BlockSpec(memory_space=pltpu.VMEM)
    return pl.pallas_call(
        functools.partial(finish_kernel, cycle, groups, tokens),
        out_shape=[
            jax.ShapeDtypeStruct((streams, cycle, share, tokens), seq.dtype),
            jax.ShapeDtypeStruct((cycle,) + last.shape, last.dtype),
            jax.ShapeDtypeStruct(small.shape, small.dtype),
        ],
        in_specs=in_any(2) + [vmem],
        out_specs=in_any(2) + [vmem],
        scratch_shapes=[
            pltpu.VMEM((cycle,) + small.shape, small.dtype),
            pltpu.VMEM(small.shape, small.dtype),
            pltpu.VMEM((groups,) + small.shape, small.dtype),
            pltpu.SemaphoreType.DMA((3, cycle)),
            pltpu.SemaphoreType.DMA((3, cycle)),
            pltpu.SemaphoreType.DMA((2,)),
            pltpu.SemaphoreType.DMA((groups,)),
            pltpu.SemaphoreType.DMA((groups,)),
        ],
        compiler_params=pltpu.CompilerParams(collective_id=ident, has_side_effects=True),
    )(seq, last, small)


def middle_kernel(
    lines, columns, parts, tokens, share,
    terms_ref, cot_ref, in_ref, sum_ref, cot_out, out_ref,
    side_buf, half_buf, line_buf, ready,
    side_send, side_recv, line_send, line_recv, ready_send, ready_recv,
    cot_send, cot_recv, far_sem, mid_sem, near_sem, core_sem, recv_sem, own_sem,
):
    ch = lax.axis_index("ch")
    ctx = lax.axis_index("ctx")
    cycle = columns * 2
    line, side = ch // 2, lax.rem(ch, 2)
    column, core = ctx // 2, lax.rem(ctx, 2)

    def at(line_to, side_to, column_to, core_to):
        return {"ch": line_to * 2 + side_to, "ctx": column_to * 2 + core_to}

    line_peers = [lax.rem(line + s, lines) for s in range(lines)]
    column_peers = [lax.rem(column + s, columns) for s in range(columns)]
    ctx_peers = [lax.rem(ctx + s, cycle) for s in range(cycle)]
    side_peers = [side, 1 - side]
    greet(
        [at(p, side, column, core) for p in line_peers[1:]]
        + [at(line, 1 - side, column, core)]
        + [{"ctx": p} for p in ctx_peers[1:]]
    )
    pending = []

    for s in [*range(1, lines), 0]:
        l = line_peers[s]
        pending.append(
            remote(
                terms_ref.at[l * 2 + 1 - side], side_buf.at[l], side_send.at[s], side_recv.at[l],
                at(line, 1 - side, column, core),
            )
        )

    def halves(s):
        l = line_peers[s]
        arrived(side_buf.at[l], side_recv.at[l])
        return terms_ref[l * 2 + side].astype(jnp.float32) + side_buf[l].astype(jnp.float32)

    def send_half(s):
        half_buf[s] = halves(s).astype(half_buf.dtype)
        pending.append(
            remote(
                half_buf.at[s], line_buf.at[line], line_send.at[s], line_recv.at[line],
                at(line_peers[s], side, column, core),
            )
        )

    def finish_sum():
        value = halves(0)
        for s in range(1, lines):
            l = line_peers[s]
            arrived(line_buf.at[l], line_recv.at[l])
            value = value + line_buf[l].astype(jnp.float32)
        value = value.astype(ready.dtype)
        for j in range(cycle):
            ready[j] = value[j * share : (j + 1) * share]
        place = sum_ref.at[:, pl.ds(pl.multiple_of(ctx * tokens, tokens), tokens)]
        copies = [
            remote(
                ready.at[ctx_peers[s]], place, ready_send.at[s], ready_recv.at[s],
                {"ctx": ctx_peers[s]},
            )
            for s in range(1, cycle)
        ]
        own = pltpu.make_async_copy(ready.at[ctx], place, own_sem.at[1])
        own.start()
        return copies + [own]

    def cot_place(j):
        return cot_out.at[:, pl.ds(pl.multiple_of(j * tokens, tokens), tokens)]

    for s in range(1, columns):
        pending.append(
            remote(
                cot_ref, cot_place(ctx), cot_send.at[0, s], cot_recv.at[ctx],
                at(line, side, column_peers[s], core),
            )
        )
    owns = [pltpu.make_async_copy(cot_ref, cot_place(ctx), own_sem.at[2])]
    owns[0].start()

    def pass_cot(s):
        j = column_peers[s] * 2 + core
        if s:
            arrived(cot_place(j), cot_recv.at[j])
        pending.append(
            remote(
                cot_place(j) if s else cot_ref, cot_place(j), cot_send.at[1, s], cot_recv.at[j],
                at(line, side, column, 1 - core),
            )
        )

    def chunk(i, j, part):
        first, rows = parts[part]
        return out_ref.at[i, j, pl.ds(first, rows)]

    def send(l, s, c, part, src, sem, target):
        i, j = l * 2 + s, c * 2 + core
        dst = chunk(i, j, part)
        pending.append(remote(dst if src is None else src, dst, sem, recv_sem.at[i, j, part], target))

    sizes = [(2, columns), (columns, 2)]

    def coords(part, u, v):
        return (side_peers[u], column_peers[v]) if part == 0 else (side_peers[v], column_peers[u])

    def pass_on(part, l, u, v, src):
        s, c = coords(part, u, v)
        lp = line_peers[l]
        size_u, size_v = sizes[part]
        if u == 0 and v == 0:
            for w in range(1, size_u):
                ts, tc = coords(part, w, 0)
                send(lp, s, c, part, src, mid_sem.at[part, l, w], at(line, ts, tc, core))
        if v == 0:
            for w in range(1, size_v):
                ts, tc = coords(part, 0, w)
                send(lp, s, c, part, src, near_sem.at[part, l, u, w], at(line, ts, tc, core))
        send(lp, s, c, part, src, core_sem.at[part, l, u, v], at(line, side, column, 1 - core))

    def wait_for(part, l, u, v):
        s, c = coords(part, u, v)
        i, j = line_peers[l] * 2 + s, c * 2 + core
        arrived(chunk(i, j, part), recv_sem.at[i, j, part])

    if parts:
        own = pltpu.make_async_copy(in_ref, out_ref.at[ch, ctx], own_sem.at[0])
        own.start()
        owns.append(own)
    for part, (first, rows) in enumerate(parts):
        mine = in_ref.at[pl.ds(first, rows)]
        for s in range(1, lines):
            send(
                line, side, column, part, mine, far_sem.at[part, s],
                at(line_peers[s], side, column, core),
            )
    pass_cot(0)
    for l in range(lines):
        for part, (first, rows) in enumerate(parts):
            if l:
                wait_for(part, l, 0, 0)
            pass_on(part, l, 0, 0, None if l else in_ref.at[pl.ds(first, rows)])
        if l + 1 < lines:
            send_half(l + 1)
    for s in range(1, columns):
        pass_cot(s)
    for l in range(lines):
        for part in range(len(parts)):
            for u in range(1, sizes[part][0]):
                wait_for(part, l, u, 0)
                pass_on(part, l, u, 0, None)
    sums = finish_sum()
    for l in range(lines):
        for part in range(len(parts)):
            for u in range(sizes[part][0]):
                for v in range(1, sizes[part][1]):
                    wait_for(part, l, u, v)
                    pass_on(part, l, u, v, None)
    for copy in owns + sums:
        copy.wait()
    for s in range(columns):
        j = column_peers[s] * 2 + 1 - core
        arrived(cot_place(j), cot_recv.at[j])
    for part in range(len(parts)):
        for l in range(lines):
            for s in range(2):
                for c in range(columns):
                    i, j = line_peers[l] * 2 + side_peers[s], column_peers[c] * 2 + (1 - core)
                    arrived(chunk(i, j, part), recv_sem.at[i, j, part])
    for copy in pending:
        copy.wait_send()


def middle(ident, terms, cot, block):
    groups, cycle = lax.axis_size("ch"), lax.axis_size("ctx")
    _, channels, tokens = terms.shape
    share, length = block.shape
    lines, columns = groups // 2, cycle // 2
    cut = share // 16 * 13 // 16 * 16
    parts = [(0, cut), (cut, share - cut)] if 0 < cut < share else [(0, share)]
    if groups * cycle > 64:
        parts = []
    most = max(2, columns)
    count = max(1, len(parts))
    spread_shape = (groups, cycle, share, length) if parts else (1, 1, 8, 128)
    dma = pltpu.SemaphoreType.DMA
    summed, cot_all, spread = pl.pallas_call(
        functools.partial(middle_kernel, lines, columns, parts, tokens, share),
        out_shape=[
            jax.ShapeDtypeStruct((share, length), terms.dtype),
            jax.ShapeDtypeStruct((cot.shape[0], length), cot.dtype),
            jax.ShapeDtypeStruct(spread_shape, block.dtype),
        ],
        in_specs=[pl.BlockSpec(memory_space=pltpu.VMEM)] + in_any(2),
        out_specs=in_any(3),
        scratch_shapes=[
            pltpu.VMEM((lines, channels, tokens), terms.dtype),
            pltpu.VMEM((lines, channels, tokens), terms.dtype),
            pltpu.VMEM((lines, channels, tokens), terms.dtype),
            pltpu.VMEM((cycle, share, tokens), terms.dtype),
            dma((lines,)),
            dma((lines,)),
            dma((lines,)),
            dma((lines,)),
            dma((cycle,)),
            dma((cycle,)),
            dma((2, columns)),
            dma((cycle,)),
            dma((count, lines)),
            dma((count, lines, most)),
            dma((count, lines, most, most)),
            dma((count, lines, most, most)),
            dma((groups if parts else 1, cycle, count)),
            dma((3,)),
        ],
        compiler_params=pltpu.CompilerParams(
            collective_id=ident, has_side_effects=True, vmem_limit_bytes=48 * 2**20
        ),
    )(terms, cot, block)
    if not parts:
        spread = lax.all_gather(lax.all_gather(block, "ctx"), "ch")
    return summed, cot_all, spread


def filter_values(filter_in, filter_mid, filter_out, decay_rate, length):
    band_count = filter_in.shape[0] // 2
    lag_index = np.arange(length)
    phases = 2.0 * math.pi / length * (np.arange(1, band_count + 1)[:, None] * lag_index % length)
    features = jnp.asarray(np.concatenate([np.cos(phases), np.sin(phases)]), jnp.float32)
    hidden_one = jnp.sin(jnp.einsum("fh,fs->hs", filter_in, features, precision=precise))
    hidden_two = jnp.sin(jnp.einsum("gh,gs->hs", filter_mid, hidden_one, precision=precise))
    raw_out = jnp.einsum("hc,hs->cs", filter_out, hidden_two, precision=precise)
    lag_axis = jnp.arange(length).astype(jnp.float32)
    return (
        raw_out * jnp.exp(-decay_rate[:, None] * lag_axis[None, :]) * jnp.sqrt(decay_rate)[:, None]
    )


def fourier_tables(width):
    double = 2 * width
    row, col = np.arange(width), np.arange(double)
    phase = 2.0 * math.pi / double * (row[:, None] * row[None, :] % double)
    forward_cos = np.cos(phase)
    forward_sin = np.where(row[None, :] == 0, (1 - 2 * (row % 2))[:, None], -np.sin(phase))
    phase = 2.0 * math.pi / double * (row[:, None] * col[None, :] % double)
    inverse_cos = np.where(row == 0, 1.0, 2.0)[:, None] / double * np.cos(phase)
    inverse_sin = np.where(
        row[:, None] == 0, (1 - 2 * (col % 2))[None, :] / double, -2.0 / double * np.sin(phase)
    )
    return (
        np.concatenate([forward_cos, forward_sin], axis=1).astype(np.float32),
        np.concatenate([inverse_cos, inverse_sin], axis=0).astype(np.float32),
    )


def spectral_product(left, right, width):
    lr, li = left[..., :width], left[..., width:]
    rr, ri = right[..., :width], right[..., width:]
    edge = lax.broadcasted_iota(jnp.int32, lr.shape, lr.ndim - 1) == 0
    cross = li * ri
    real = lr * rr - jnp.where(edge, 0.0, cross)
    imag = jnp.where(edge, cross, lr * ri + li * rr)
    return jnp.concatenate([real, imag], axis=-1)


def spectral_adjoint(left, right, width):
    lr, li = left[..., :width], left[..., width:]
    rr, ri = right[..., :width], right[..., width:]
    edge = lax.broadcasted_iota(jnp.int32, lr.shape, lr.ndim - 1) == 0
    cross = li * ri
    real = lr * rr + jnp.where(edge, 0.0, cross)
    imag = jnp.where(edge, cross, lr * ri - li * rr)
    return jnp.concatenate([real, imag], axis=-1)


def to_blocks(signal, blocks, width):
    return [signal[:, n * width : (n + 1) * width] for n in range(blocks)]


def transform(values, table):
    return jnp.dot(values, table, precision=precise)


def total(terms):
    terms = list(terms)
    value = terms[0]
    for term in terms[1:]:
        value = value + term
    return value


def short_apply(signal, taps):
    wide = signal.astype(jnp.float32)
    out = taps[..., 0:1] * wide
    for lag in range(1, taps.shape[-1]):
        moved = jnp.pad(wide, ((0, 0), (0, 0), (lag, 0)))[:, :, : wide.shape[2]]
        out = out + taps[..., lag : lag + 1] * moved
    return out


def short_adjoint(signal, taps):
    out = taps[..., 0:1] * signal
    for lag in range(1, taps.shape[-1]):
        moved = jnp.pad(signal, ((0, 0), (0, 0), (0, lag)))[:, :, lag:]
        out = out + taps[..., lag : lag + 1] * moved
    return out


def shards(
    streams,
    short_taps,
    filter_in,
    filter_mid,
    filter_out,
    decay_rate,
    skip_gain,
    out_weight,
    grad_out,
):
    channels, tokens = streams.shape[1:]
    cycle, groups = lax.axis_size("ctx"), lax.axis_size("ch")
    ctx = lax.axis_index("ctx")
    length = tokens * cycle
    share = channels // cycle
    width = min(256, tokens)
    blocks = length // width
    forward, inverse = fourier_tables(width)

    def mine(value, axis):
        return lax.dynamic_slice_in_dim(value, ctx * share, share, axis)

    whole = to_sequence(0, streams.reshape(3, cycle, share, tokens))
    terms = jnp.einsum("dc,dt->ct", out_weight, grad_out, preferred_element_type=jnp.float32)
    terms = terms.astype(jnp.bfloat16).reshape(groups, channels, tokens)

    taps = mine(short_taps, 1)
    skip = mine(skip_gain, 0)[:, None]
    rate = mine(decay_rate, 0)

    def make_filter(first_w, middle_w, last_w):
        return filter_values(first_w, middle_w, last_w, rate, length)

    long_filter, pullback = jax.vjp(make_filter, filter_in, filter_mid, mine(filter_out, 1))
    filtered = short_apply(whole, taps)
    product = (filtered[1] * filtered[2]).astype(jnp.bfloat16).astype(jnp.float32)

    lag_spec = [transform(b, forward) for b in to_blocks(long_filter, blocks, width)]
    own_spec = [transform(b, forward) for b in to_blocks(product, blocks, width)]
    out_blocks = []
    carry = 0.0
    for k in range(blocks):
        spec = total(spectral_product(lag_spec[i], own_spec[k - i], width) for i in range(k + 1))
        double = transform(spec, inverse)
        out_blocks.append(double[:, :width] + carry)
        carry = double[:, width:]
    long_out = jnp.concatenate(out_blocks, axis=1) + skip * product
    gated_out = (filtered[0] * long_out).astype(jnp.bfloat16)

    grad_gated, grad_all, gated = middle(1, terms, grad_out, gated_out)
    gated = gated.reshape(groups * channels, length)
    here = lax.dynamic_slice_in_dim(gated, ctx * tokens, tokens, 1)
    layer_out = jnp.dot(out_weight, here, preferred_element_type=jnp.float32).astype(jnp.bfloat16)
    weight_grad = jnp.einsum("dt,ct->dc", grad_all, gated, preferred_element_type=jnp.float32)

    grad_gated = grad_gated.astype(jnp.float32)
    grad_long = (grad_gated * filtered[0]).astype(jnp.bfloat16).astype(jnp.float32)
    grad_first = grad_gated * long_out
    grad_blocks = to_blocks(grad_long, blocks, width)
    grad_spec = []
    for k in range(blocks):
        after = grad_blocks[k + 1] if k + 1 < blocks else jnp.zeros_like(grad_blocks[k])
        grad_spec.append(transform(jnp.concatenate([grad_blocks[k], after], axis=1), inverse.T))
    back_blocks, lag_blocks = [], []
    for j in range(blocks):
        back = total(spectral_adjoint(lag_spec[k - j], grad_spec[k], width) for k in range(j, blocks))
        lags = total(spectral_adjoint(own_spec[k - j], grad_spec[k], width) for k in range(j, blocks))
        back_blocks.append(transform(back, forward.T))
        lag_blocks.append(transform(lags, forward.T))
    grad_product = jnp.concatenate(back_blocks, axis=1) + skip * grad_long
    grad_lag = jnp.concatenate(lag_blocks, axis=1)
    grad_filtered = jnp.stack([grad_first, grad_product * filtered[2], grad_product * filtered[1]])
    grad_streams = short_adjoint(grad_filtered, taps).astype(jnp.bfloat16)
    grad_in, grad_mid, grad_last = pullback(grad_lag)

    small = jnp.concatenate([grad_in, grad_mid], axis=0).reshape(-1, 128)
    grad_streams, grad_last, small = finish(2, grad_streams, grad_last.T, small, tokens)
    grad_streams = grad_streams.reshape(streams.shape)
    grad_filter_out = grad_last.reshape(channels, filter_out.shape[0]).T
    small = small.reshape(-1, filter_in.shape[1])
    cut = filter_in.shape[0]
    return (layer_out, grad_streams, small[:cut], small[cut:], grad_filter_out, weight_grad)


def solution(mesh):
    return jax.shard_map(
        shards,
        mesh=mesh,
        in_specs=(
            P(None, "ch", "ctx"),
            P(None, "ch", None),
            P(),
            P(),
            P(None, "ch"),
            P("ch"),
            P("ch"),
            P("ch", None),
            P("ch", "ctx"),
        ),
        out_specs=(P("ch", "ctx"), P(None, "ch", "ctx"), P(), P(), P(None, "ch"), P("ch", None)),
        check_vma=False,
    )
```

profile of v0, /device:TPU:0, one launch (start us, length us, event | category | flops | bytes accessed | tf_op | source)
XLA Modules:
  0.0 189.5 jit_solution(6786163008303911125)
XLA Ops:
  0.6 4.7 %convolution_convert_fusion = bf16[4608,256]{1,0:T(8,128)(2,1)S(1)} fusion(bf16[576,4608]{1,0:T(8,128)(2,1)} %param.31, bf16[576,256]{1,0:T(8,128)(2,1)} %cot_ref.1), kind=kOutput, calls=%fused_computation | convolution fusion | flops 1360134144 | bytes 7962624 | tf_op jit(solution)/shard_map/dc,dt->ct/dot_general | solution.py:480
  5.3 13.4 %shard_map.271 = bf16[3,144,1024]{2,1,0:T(8,128)(2,1)} custom-call(bf16[3,4,144,256]{3,2,1,0:T(8,128)(2,1)} %bitcast.93), custom_call_target="tpu_custom_call" | custom-call | tf_op jit(solution)/shard_map/pallas_call | solution.py:62
  18.7 2.6 %convert_element_type.49 = f32[3,144,1024]{2,1,0:T(8,128)} convert(bf16[3,144,1024]{2,1,0:T(8,128)(2,1)} %shard_map.271) | non-fusion elementwise | flops 442368 | bytes 2654208 | tf_op jit(solution)/shard_map/convert_element_type | solution.py:440
  21.3 0.9 constant_dynamic-slice_fusion.1
  22.3 4.1 %fusion.4 = f32[3,144,1024]{2,1,0:T(8,128)S(1)} fusion(f32[3,144,1024]{2,1,0:T(8,128)} %convert_element_type.49, f32[3,144]{1,0:T(4,128)S(1)} %get-tuple-element.114, f32[3,144]{1,0:T(4,128)S(1)} %get-tuple-element.115, f32[3,144]{1,0:T(4,128)S(1)} %bitcast.97), kind=kLoop, calls=%fused_computation.9 | loop fusion | flops 2211840 | bytes 3544128 | tf_op jit(solution)/shard_map/add | solution.py:444
  26.5 0.9 dynamic_slice.18
  27.4 1.9 %fusion.226 = (f32[1024,64]{0,1:T(8,128)S(1)}, f32[1024,64]{0,1:T(8,128)}) fusion(f32[32,1024]{1,0:T(8,128)S(1)} %copy-done.38, f32[32,64]{1,0:T(8,128)S(1)} %copy-done.53), kind=kOutput, calls=%fused_computation.334 | convolution fusion | flops 25165824 | bytes 663552 | tf_op jit(solution)/shard_map/jvp(fh,fs->hs)/dot_general | solution.py:377
  29.3 1.9 %fusion.227 = (f32[1024,64]{0,1:T(8,128)S(1)}, f32[1024,64]{0,1:T(8,128)}) fusion(f32[1024,64]{0,1:T(8,128)S(1)} %get-tuple-element.110, f32[64,64]{1,0:T(8,128)S(1)} %copy-done.43), kind=kOutput, calls=%fused_computation.335 | convolution fusion | flops 50331648 | bytes 802816 | tf_op jit(solution)/shard_map/jvp(gh,gs->hs)/dot_general | solution.py:378
  31.2 0.8 dynamic-slice_negate_fusion
  32.0 0.8 fusion.11
  37.7 0.8 fusion.29
  39.0 0.6 fusion.153
  40.2 0.8 fusion.22
  41.9 75.6 %shard_map.272 = (bf16[144,1024]{1,0:T(8,128)(2,1)S(1)}, bf16[576,1024]{1,0:T(8,128)(2,1)S(1)}, bf16[8,4,144,1024]{3,2,1,0:T(8,128)(2,1)}) custom-call(bf16[8,576,256]{2,1,0:T(8,128)(2,1)S(1)} %bitcast.92, bf16[576,256]{1,0:T(8,128)(2,1)S(1)} %copy-done.1, bf16[144,1024]{1,0:T(8,128)(2,1)S(1)} %multiply_convert_fusion.in_ref), custom_call_target="tpu_custom_call" | custom-call | tf_op jit(solution)/shard_map/pallas_call | solution.py:334
  117.5 1.0 copy-done.2
  118.6 5.6 %fusion.15 = bf16[576,256]{1,0:T(8,128)(2,1)} fusion(bf16[576,4608]{1,0:T(8,128)(2,1)} %param.31, bf16[4608,1024]{1,0:T(8,128)(2,1)} %bitcast.99, s32[]{:T(128)S(6)} %select_n.212), kind=kOutput, calls=%fused_computation.20 | convolution fusion | flops 1359101952 | bytes 7962628 | tf_op jit(solution)/shard_map/dot_general | solution.py:509
  124.5 1.0 copy-done.8
  125.5 0.8 fusion.117
  130.3 0.8 copy-done.14
  133.8 2.3 %fusion.9.seq_ref = bf16[3,144,1024]{2,1,0:T(8,128)(2,1)} fusion(f32[3,144,1024]{2,1,0:T(8,128)S(1)} %pad_maximum_fusion, f32[3,144]{1,0:T(4,128)S(1)} %copy-done.46, f32[3,144]{1,0:T(4,128)S(1)} %copy-done.48, f32[3,144]{1,0:T(4,128)S(1)} %bitcast.98), kind=kLoop, calls=%fused_computation.14 | loop fusion | flops 2654208 | bytes 2659392 | tf_op jit(solution)/shard_map/convert_element_type | solution.py:529
  138.4 1.4 fusion.223.last_ref
  139.8 1.6 convolution_multiply_fusion.2
  141.8 1.2 convolution_multiply_fusion.1
  143.6 0.7 reshape.44.small_ref
  144.3 27.7 %shard_map.273 = (bf16[3,4,144,256]{3,2,1,0:T(8,128)(2,1)}, f32[4,144,64]{2,1,0:T(8,128)}, f32[48,128]{1,0:T(8,128)}) custom-call(bf16[3,144,1024]{2,1,0:T(8,128)(2,1)} %fusion.9.seq_ref, f32[144,64]{1,0:T(8,128)} %fusion.223.last_ref, f32[48,128]{1,0:T(8,128)} %reshape.44.small_ref), custom_call_target="tpu_custom_call" | custom-call | tf_op jit(solution)/shard_map/pallas_call | solution.py:122
  172.0 0.7 slice.320
  172.7 0.7 slice.321
  173.4 0.7 slice.322
  174.1 0.7 slice.323
  174.8 1.8 copy.37
  176.6 12.0 %fusion.230 = f32[576,4608]{1,0:T(8,128)} fusion(bf16[576,1024]{1,0:T(8,128)(2,1)S(1)} %copy-done.3, bf16[4608,1024]{1,0:T(8,128)(2,1)} %bitcast.100), kind=kOutput, calls=%fused_computation.338 | convolution fusion | flops 5435817984 | bytes 21233664 | tf_op jit(solution)/shard_map/dt,ct->dc/dot_general | solution.py:510
  188.6 0.9 copy.48
  (169 shorter events, 16.5 us)
Async XLA Ops:
  0.6 31.3 %copy-start = (f32[64,576]{1,0:T(8,128)S(1)}, f32[64,576]{1,0:T(8,128)}, u32[]{:S(2)}) copy-start(f32[64,576]{1,0:T(8,128)} %param.28) | copy-start | bytes 442372
  22.2 4.2 %copy-start.45 = (f32[3,144]{1,0:T(4,128)}, f32[3,144]{1,0:T(4,128)S(1)}, u32[]{:S(2)}) copy-start(f32[3,144]{1,0:T(4,128)S(1)} %get-tuple-element.114) | copy-start | bytes 5188
  22.2 4.2 %copy-start.47 = (f32[3,144]{1,0:T(4,128)}, f32[3,144]{1,0:T(4,128)S(1)}, u32[]{:S(2)}) copy-start(f32[3,144]{1,0:T(4,128)S(1)} %get-tuple-element.115) | copy-start | bytes 5188
  22.3 4.2 %copy-start.49 = (f32[3,144,1]{1,0,2:T(4,128)}, f32[3,144,1]{1,0,2:T(4,128)S(1)}, u32[]{:S(2)}) copy-start(f32[3,144,1]{1,0,2:T(4,128)S(1)} %copy.46) | copy-start | bytes 5188
  22.3 5.1 %copy-start.38 = (f32[32,1024]{1,0:T(8,128)S(1)}, f32[32,1024]{1,0:T(8,128)}, u32[]{:S(2)}) copy-start(f32[32,1024]{1,0:T(8,128)} %constant.30.clone) | copy-start | bytes 393220
  22.3 5.1 %copy-start.53 = (f32[32,64]{1,0:T(8,128)S(1)}, f32[32,64]{1,0:T(8,128)}, u32[]{:S(2)}) copy-start(f32[32,64]{1,0:T(8,128)} %param.26) | copy-start | bytes 24580
  22.3 7.0 %copy-start.43 = (f32[64,64]{1,0:T(8,128)S(1)}, f32[64,64]{1,0:T(8,128)}, u32[]{:S(2)}) copy-start(f32[64,64]{1,0:T(8,128)} %param.27) | copy-start | bytes 49156
  26.4 14.6 %copy-start.5 = (f32[3,144,1024]{2,1,0:T(8,128)}, f32[3,144,1024]{2,1,0:T(8,128)S(1)}, u32[]{:S(2)}) copy-start(f32[3,144,1024]{2,1,0:T(8,128)S(1)} %fusion.4) | copy-start | bytes 5308420
  26.5 6.3 %copy-start.4 = (f32[256,512]{1,0:T(8,128)S(1)}, f32[256,512]{1,0:T(8,128)}, u32[]{:S(2)}) copy-start(f32[256,512]{1,0:T(8,128)} %constant.31.clone) | copy-start | bytes 1572868
  27.3 13.7 %copy-start.54 = (f32[144]{0:T(256)}, f32[144]{0:T(256)S(1)}, u32[]{:S(2)}) copy-start(f32[144]{0:T(256)S(1)} %dynamic_slice.18) | copy-start | bytes 1732
  29.3 2.7 %copy-start.22 = (f32[1024,64]{0,1:T(8,128)}, f32[1024,64]{0,1:T(8,128)S(1)}, u32[]{:S(2)}) copy-start(f32[1024,64]{0,1:T(8,128)S(1)} %get-tuple-element.110) | copy-start | bytes 786436
  31.2 2.1 %copy-start.30 = (f32[1024,64]{0,1:T(8,128)}, f32[1024,64]{0,1:T(8,128)S(1)}, u32[]{:S(2)}) copy-start(f32[1024,64]{0,1:T(8,128)S(1)} %get-tuple-element.112) | copy-start | bytes 786436
  33.2 3.1 %copy-start.15 = (f32[144,512]{1,0:T(8,128)}, f32[144,512]{1,0:T(8,128)S(1)}, u32[]{:S(2)}) copy-start(f32[144,512]{1,0:T(8,128)S(1)} %fusion.127) | copy-start | bytes 884740
  33.3 6.4 %copy-start.41 = (pred[256]{0:T(512)(128)(4,1)}, pred[256]{0:T(512)(128)(4,1)S(1)}, u32[]{:S(2)}) copy-start(pred[256]{0:T(512)(128)(4,1)S(1)} %iota_compare_fusion) | copy-start | bytes 772
  33.7 2.8 %copy-start.9 = (f32[144,512]{1,0:T(8,128)}, f32[144,512]{1,0:T(8,128)S(1)}, u32[]{:S(2)}) copy-start(f32[144,512]{1,0:T(8,128)S(1)} %fusion.161) | copy-start | bytes 884740
  35.0 1.5 copy-start.13
  39.0 2.1 %copy-start.28 = (f32[144,256]{1,0:T(8,128)}, f32[144,256]{1,0:T(8,128)S(1)}, u32[]{:S(2)}) copy-start(f32[144,256]{1,0:T(8,128)S(1)} %convolution_add_fusion.1) | copy-start | bytes 442372
  118.5 5.7 %copy-start.6 = (f32[3,144,1024]{2,1,0:T(8,128)S(1)}, f32[3,144,1024]{2,1,0:T(8,128)}, u32[]{:S(2)}) copy-start(f32[3,144,1024]{2,1,0:T(8,128)} %copy-done.5) | copy-start | bytes 5308420
  118.5 5.7 %copy-start.25 = (f32[144,256]{1,0:T(8,128)S(1)}, f32[144,256]{1,0:T(8,128)}, u32[]{:S(2)}) copy-start(f32[144,256]{1,0:T(8,128)} %copy-done.24) | copy-start | bytes 442372
  118.5 5.7 %copy-start.27 = (f32[144,256]{1,0:T(8,128)S(1)}, f32[144,256]{1,0:T(8,128)}, u32[]{:S(2)}) copy-start(f32[144,256]{1,0:T(8,128)} %copy-done.26) | copy-start | bytes 442372
  118.5 5.7 %copy-start.29 = (f32[144,256]{1,0:T(8,128)S(1)}, f32[144,256]{1,0:T(8,128)}, u32[]{:S(2)}) copy-start(f32[144,256]{1,0:T(8,128)} %copy-done.28) | copy-start | bytes 442372
  118.5 5.7 %copy-start.55 = (f32[144]{0:T(256)S(1)}, f32[144]{0:T(256)}, u32[]{:S(2)}) copy-start(f32[144]{0:T(256)} %copy-done.54) | copy-start | bytes 1732
  124.4 1.8 copy-start.34
  124.5 1.8 copy-start.42
  124.5 2.1 %copy-start.32 = (f32[256,256]{1,0:T(8,128)S(1)}, f32[256,256]{1,0:T(8,128)}, u32[]{:S(2)}) copy-start(f32[256,256]{1,0:T(8,128)} %constant.48) | copy-start | bytes 786436
  137.9 1.9 %copy-start.40 = (f32[1024,64]{0,1:T(8,128)S(1)}, f32[1024,64]{0,1:T(8,128)}, u32[]{:S(2)}) copy-start(f32[1024,64]{0,1:T(8,128)} %get-tuple-element.113) | copy-start | bytes 786436
  138.4 3.0 %copy-start.23 = (f32[1024,64]{0,1:T(8,128)S(1)}, f32[1024,64]{0,1:T(8,128)}, u32[]{:S(2)}) copy-start(f32[1024,64]{0,1:T(8,128)} %copy-done.22) | copy-start | bytes 786436
  138.4 3.4 %copy-start.33 = (f32[1024,64]{0,1:T(8,128)S(1)}, f32[1024,64]{0,1:T(8,128)}, u32[]{:S(2)}) copy-start(f32[1024,64]{0,1:T(8,128)} %get-tuple-element.111) | copy-start | bytes 786436
  138.4 3.4 %copy-start.44 = (f32[64,64]{1,0:T(8,128)S(1)}, f32[64,64]{1,0:T(8,128)}, u32[]{:S(2)}) copy-start(f32[64,64]{1,0:T(8,128)} %param.27) | copy-start | bytes 49156
  139.8 3.3 %copy-start.39 = (f32[32,1024]{1,0:T(8,128)S(1)}, f32[32,1024]{1,0:T(8,128)}, u32[]{:S(2)}) copy-start(f32[32,1024]{1,0:T(8,128)} %constant.30.clone) | copy-start | bytes 393220
  141.4 35.1 %copy-start.3 = (bf16[576,1024]{1,0:T(8,128)(2,1)S(1)}, bf16[576,1024]{1,0:T(8,128)(2,1)}, u32[]{:S(2)}) copy-start(bf16[576,1024]{1,0:T(8,128)(2,1)} %copy-done.2) | copy-start | bytes 3538948
  176.6 12.0 %copy-start.35 = (bf16[3,4,144,256]{3,2,1,0:T(8,128)(2,1)S(1)}, bf16[3,4,144,256]{3,2,1,0:T(8,128)(2,1)}, u32[]{:S(2)}) copy-start(bf16[3,4,144,256]{3,2,1,0:T(8,128)(2,1)} %get-tuple-element.14) | copy-start | bytes 2654212
  (28 other events, 28.2 us)
where the time goes:
time: 192 us; the launch traced here: 190 us
  Pallas kernels  117 us (61%)
  matrix products  44.5 us (23%)
  local copies, waits for them, and re-layouts  14.7 us (8%)
  other arithmetic  11.8 us (6%)
    pallas_call x1, Pallas kernels, middle(): pl.pallas_call(functools.partial(middle_kernel, lines, columns, parts, to...  75.6 us
    pallas_call x1, Pallas kernels, finish(): pl.pallas_call(functools.partial(finish_kernel, cycle, groups, tokens), o...  27.7 us
    pallas_call x1, Pallas kernels, to_sequence(): pl.pallas_call(functools.partial(to_sequence_kernel, cycle, tokens), out_...  13.4 us
    dot_general x27, matrix products, transform(): return jnp.dot(values, table, precision=precise)  12.6 us
    dot_general x1, matrix products, shards(): jnp.einsum('dt,ct->dc', grad_all, gated, preferred_element_type=jnp.float32)  12 us
    unnamed x123, local copies, waits for them, and re-layouts  7.6 us
    dot_general x1, matrix products, shards(): jnp.dot(out_weight, here, preferred_element_type=jnp.float32)  5.64 us
    dot_general x1, matrix products, shards(): jnp.einsum('dc,dt->ct', out_weight, grad_out, preferred_element_type=jnp....  4.65 us

commit v1 on v0

v1 whole, which is shorter than its diff:
```python
import functools
import math

import jax
import jax.numpy as jnp
import numpy as np
from jax import lax
from jax.experimental import pallas as pl
from jax.experimental.pallas import tpu as pltpu
from jax.sharding import PartitionSpec as P

precise = lax.Precision.HIGHEST
MESH = pl.DeviceIdType.MESH


def arrived(ref, sem):
    pltpu.make_async_copy(ref, ref, sem).wait()


def greet(friends):
    barrier = pltpu.get_barrier_semaphore()
    for friend in friends:
        pl.semaphore_signal(barrier, inc=1, device_id=friend, device_id_type=MESH)
    pl.semaphore_wait(barrier, len(friends))


def remote(src, dst, send_sem, recv_sem, target):
    copy = pltpu.make_async_remote_copy(
        src_ref=src,
        dst_ref=dst,
        send_sem=send_sem,
        recv_sem=recv_sem,
        device_id=target,
        device_id_type=MESH,
    )
    copy.start()
    return copy


def in_any(count):
    return [pl.BlockSpec(memory_space=pl.ANY)] * count


def layer_kernel(
    lines, columns, parts, tokens, share, width,
    streams_ref, terms_ref, cot_ref, taps_ref, skip_ref, env_ref, last_ref, last_flat_ref,
    mid_ref, one_ref, one_slope_ref, two_ref, two_slope_ref, features_ref, forward_ref, inverse_ref,
    gated_ref, cot_out, out_ref, back_out, last_out, small_out,
    seq, filtered, product, long_out, lag_spec, own_spec, sum_ref, back_seq, last_own,
    small_own, from_ctx, small_sum, from_ch,
    side_buf, half_buf, line_buf, ready,
    seq_send, seq_recv, side_send, side_recv, line_send, line_recv, ready_send, ready_recv,
    cot_send, cot_recv, far_sem, mid_sem, near_sem, core_sem, recv_sem, own_sem,
    back_send, back_recv, ch_send, ch_recv,
):
    ch = lax.axis_index("ch")
    ctx = lax.axis_index("ctx")
    cycle = columns * 2
    line, side = ch // 2, lax.rem(ch, 2)
    column, core = ctx // 2, lax.rem(ctx, 2)

    def at(line_to, side_to, column_to, core_to):
        return {"ch": line_to * 2 + side_to, "ctx": column_to * 2 + core_to}

    line_peers = [lax.rem(line + s, lines) for s in range(lines)]
    column_peers = [lax.rem(column + s, columns) for s in range(columns)]
    ctx_peers = [lax.rem(ctx + s, cycle) for s in range(cycle)]
    side_peers = [side, 1 - side]
    groups = lines * 2
    ch_peers = [lax.rem(ch + s, groups) for s in range(groups)]
    greet([{"ctx": p} for p in ctx_peers[1:]] + [{"ch": p} for p in ch_peers[1:]])
    pending = []
    blocks = cycle * tokens // width

    def span(j):
        return pl.ds(pl.multiple_of(j * tokens, tokens), tokens)

    seq_copies = [
        remote(
            streams_ref.at[:, ctx_peers[s]], seq.at[:, :, span(ctx)], seq_send.at[s], seq_recv.at[s],
            {"ctx": ctx_peers[s]},
        )
        for s in range(1, cycle)
    ]
    seq_copies.append(
        pltpu.make_async_copy(streams_ref.at[:, ctx], seq.at[:, :, span(ctx)], own_sem.at[3])
    )
    seq_copies[-1].start()

    for s in [*range(1, lines), 0]:
        l = line_peers[s]
        pending.append(
            remote(
                terms_ref.at[l * 2 + 1 - side], side_buf.at[l], side_send.at[s], side_recv.at[l],
                at(line, 1 - side, column, core),
            )
        )

    def halves(s):
        l = line_peers[s]
        arrived(side_buf.at[l], side_recv.at[l])
        return terms_ref[l * 2 + side].astype(jnp.float32) + side_buf[l].astype(jnp.float32)

    def send_half(s):
        half_buf[s] = halves(s).astype(half_buf.dtype)
        pending.append(
            remote(
                half_buf.at[s], line_buf.at[line], line_send.at[s], line_recv.at[line],
                at(line_peers[s], side, column, core),
            )
        )

    def finish_sum():
        value = halves(0)
        for s in range(1, lines):
            l = line_peers[s]
            arrived(line_buf.at[l], line_recv.at[l])
            value = value + line_buf[l].astype(jnp.float32)
        value = value.astype(ready.dtype)
        if ready.shape[1] != share:
            ready[...] = jnp.zeros(ready.shape, ready.dtype)
        for j in range(cycle):
            ready[j, :share] = value[j * share : (j + 1) * share]
        place = sum_ref.at[:, pl.ds(pl.multiple_of(ctx * tokens, tokens), tokens)]
        copies = [
            remote(
                ready.at[ctx_peers[s]], place, ready_send.at[s], ready_recv.at[s],
                {"ctx": ctx_peers[s]},
            )
            for s in range(1, cycle)
        ]
        own = pltpu.make_async_copy(ready.at[ctx], place, own_sem.at[1])
        own.start()
        return copies + [own]

    def cot_place(j):
        return cot_out.at[:, pl.ds(pl.multiple_of(j * tokens, tokens), tokens)]

    for s in range(1, columns):
        pending.append(
            remote(
                cot_ref, cot_place(ctx), cot_send.at[0, s], cot_recv.at[ctx],
                at(line, side, column_peers[s], core),
            )
        )
    owns = [pltpu.make_async_copy(cot_ref, cot_place(ctx), own_sem.at[2])]
    owns[0].start()

    def pass_cot(s):
        j = column_peers[s] * 2 + core
        if s:
            arrived(cot_place(j), cot_recv.at[j])
        pending.append(
            remote(
                cot_place(j) if s else cot_ref, cot_place(j), cot_send.at[1, s], cot_recv.at[j],
                at(line, side, column, 1 - core),
            )
        )

    def chunk(i, j, part):
        first, rows = parts[part]
        return out_ref.at[i, j, pl.ds(first, rows)]

    def send(l, s, c, part, src, sem, target):
        i, j = l * 2 + s, c * 2 + core
        dst = chunk(i, j, part)
        pending.append(remote(dst if src is None else src, dst, sem, recv_sem.at[i, j, part], target))

    sizes = [(2, columns), (columns, 2)]

    def coords(part, u, v):
        return (side_peers[u], column_peers[v]) if part == 0 else (side_peers[v], column_peers[u])

    def pass_on(part, l, u, v, src):
        s, c = coords(part, u, v)
        lp = line_peers[l]
        size_u, size_v = sizes[part]
        if u == 0 and v == 0:
            for w in range(1, size_u):
                ts, tc = coords(part, w, 0)
                send(lp, s, c, part, src, mid_sem.at[part, l, w], at(line, ts, tc, core))
        if v == 0:
            for w in range(1, size_v):
                ts, tc = coords(part, 0, w)
                send(lp, s, c, part, src, near_sem.at[part, l, u, w], at(line, ts, tc, core))
        send(lp, s, c, part, src, core_sem.at[part, l, u, v], at(line, side, column, 1 - core))

    def wait_for(part, l, u, v):
        s, c = coords(part, u, v)
        i, j = line_peers[l] * 2 + s, c * 2 + core
        arrived(chunk(i, j, part), recv_sem.at[i, j, part])

    def start_spread():
        if parts:
            own = pltpu.make_async_copy(gated_ref, out_ref.at[ch, ctx], own_sem.at[0])
            own.start()
            owns.append(own)
        for part, (first, rows) in enumerate(parts):
            mine = gated_ref.at[pl.ds(first, rows)]
            for s in range(1, lines):
                send(
                    line, side, column, part, mine, far_sem.at[part, s],
                    at(line_peers[s], side, column, core),
                )

    def cut(value):
        return jnp.concatenate([value[:, n * width : (n + 1) * width] for n in range(blocks)], axis=0)

    def glue(value):
        rows = value.shape[0] // blocks
        return jnp.concatenate([value[n * rows : (n + 1) * rows] for n in range(blocks)], axis=1)

    def dot(left, right, dims=((1,), (0,))):
        return lax.dot_general(
            left, right, (dims, ((), ())), precision=precise, preferred_element_type=jnp.float32
        )

    rows = gated_ref.shape[0]
    flat = ((1,), (1,))
    pass_cot(0)
    lag_spec[...] = dot(cut(dot(last_ref[...], two_ref[...]) * env_ref[...]), forward_ref[...])
    if lines > 1:
        send_half(1)
    for copy in seq_copies:
        copy.wait()
    if lines > 2:
        send_half(2)
    for n in range(3):
        filtered[n] = short_apply(seq[n].astype(jnp.float32), taps_ref[n])
    wide = (filtered[1] * filtered[2]).astype(jnp.bfloat16).astype(jnp.float32)
    product[...] = wide
    own_spec[...] = dot(cut(wide), forward_ref[...])

    def at_block(ref, n):
        return ref[n * rows : (n + 1) * rows]

    specs = [
        total(
            spectral_product(at_block(lag_spec, i), at_block(own_spec, k - i), width)
            for i in range(k + 1)
        )
        for k in range(blocks)
    ]
    double = dot(jnp.concatenate(specs, axis=0), inverse_ref[...])
    carry = jnp.concatenate(
        [jnp.zeros((rows, width), jnp.float32), double[: (blocks - 1) * rows, width:]], axis=0
    )
    value = glue(double[:, :width] + carry) + skip_ref[...] * product[...]
    long_out[...] = value
    gated_ref[...] = (filtered[0] * value).astype(gated_ref.dtype)

    start_spread()
    for l in range(lines):
        for part, (first, size) in enumerate(parts):
            if l:
                wait_for(part, l, 0, 0)
            pass_on(part, l, 0, 0, None if l else gated_ref.at[pl.ds(first, size)])
        if 2 < l + 3 < lines:
            send_half(l + 3)

    def second(l):
        for part in range(len(parts)):
            for u in range(1, sizes[part][0]):
                wait_for(part, l, u, 0)
                pass_on(part, l, u, 0, None)

    for s in range(1, columns):
        pass_cot(s)
    second(0)
    sums = finish_sum()
    for l in range(1, lines // 2):
        second(l)
    for copy in sums:
        copy.wait()

    cotangent = sum_ref[...].astype(jnp.float32)
    grad_long = (cotangent * filtered[0]).astype(jnp.bfloat16).astype(jnp.float32)
    stacked = cut(grad_long)
    after = jnp.concatenate([stacked[rows:], jnp.zeros((rows, width), jnp.float32)], axis=0)
    grad_spec = dot(jnp.concatenate([stacked, after], axis=1), inverse_ref[...], flat)

    def adjoint(ref):
        found = [
            total(
                spectral_adjoint(at_block(ref, k - j), grad_spec[k * rows : (k + 1) * rows], width)
                for k in range(j, blocks)
            )
            for j in range(blocks)
        ]
        return glue(dot(jnp.concatenate(found, axis=0), forward_ref[...], flat))

    grad_product = adjoint(lag_spec) + skip_ref[...] * grad_long
    grads = [cotangent * long_out[...], grad_product * filtered[2], grad_product * filtered[1]]
    for n in range(3):
        back_seq[n] = short_adjoint(grads[n], taps_ref[n]).astype(back_seq.dtype)
    backs = [
        remote(
            back_seq.at[:, :, span(ctx_peers[s])], back_out.at[:, ctx],
            back_send.at[0, s], back_recv.at[0, s], {"ctx": ctx_peers[s]},
        )
        for s in range(1, cycle)
    ]
    backs.append(
        pltpu.make_async_copy(back_seq.at[:, :, span(ctx)], back_out.at[:, ctx], own_sem.at[4])
    )
    backs[-1].start()
    for l in range(max(1, lines // 2), lines):
        second(l)

    grad_raw = adjoint(own_spec) * env_ref[...]
    last_own[...] = dot(grad_raw, two_ref[...], flat)
    slope = dot(last_flat_ref[...], grad_raw) * two_slope_ref[...]
    bands = features_ref.shape[0]
    small_own[bands:] = dot(one_ref[...], slope, flat)
    slope = dot(mid_ref[...], slope) * one_slope_ref[...]
    small_own[:bands] = dot(features_ref[...], slope, flat)
    smalls = []
    for s in range(1, cycle):
        to = {"ctx": ctx_peers[s]}
        smalls.append(
            remote(small_own, from_ctx.at[ctx], back_send.at[1, s], back_recv.at[1, s], to)
        )
        backs.append(
            remote(last_own, last_out.at[ctx], back_send.at[2, s], back_recv.at[2, s], to)
        )
    backs.append(pltpu.make_async_copy(last_own, last_out.at[ctx], own_sem.at[5]))
    backs[-1].start()
    from_ctx[ctx] = small_own[...]
    for copy in smalls:
        copy.wait()
    small_sum[...] = total(from_ctx[j] for j in range(cycle))
    smalls = [
        remote(small_sum, from_ch.at[ch], ch_send.at[s], ch_recv.at[s], {"ch": ch_peers[s]})
        for s in range(1, groups)
    ]
    for l in range(lines):
        for part in range(len(parts)):
            for u in range(sizes[part][0]):
                for v in range(1, sizes[part][1]):
                    wait_for(part, l, u, v)
                    pass_on(part, l, u, v, None)
    from_ch[ch] = small_sum[...]
    for copy in smalls:
        copy.wait()
    small_out[...] = total(from_ch[i] for i in range(groups))
    for copy in owns + backs:
        copy.wait()
    for s in range(columns):
        j = column_peers[s] * 2 + 1 - core
        arrived(cot_place(j), cot_recv.at[j])
    for part in range(len(parts)):
        for l in range(lines):
            for s in range(2):
                for c in range(columns):
                    i, j = line_peers[l] * 2 + side_peers[s], column_peers[c] * 2 + (1 - core)
                    arrived(chunk(i, j, part), recv_sem.at[i, j, part])
    for copy in pending:
        copy.wait_send()


def layer(ident, streams, terms, cot, taps, skip, env, last, mid, hidden, features, share):
    groups, cycle = lax.axis_size("ch"), lax.axis_size("ctx")
    _, channels, tokens = terms.shape
    rows, length = env.shape
    width = min(256, tokens)
    blocks = length // width
    lines, columns = groups // 2, cycle // 2
    cut = share // 16 * 13 // 16 * 16
    parts = [(0, cut), (cut, share - cut)] if 0 < cut < share else [(0, share)]
    if groups * cycle > 64:
        parts = []
    most = max(2, columns)
    count = max(1, len(parts))
    spread_shape = (groups, cycle, rows, length) if parts else (1, 1, 16, 128)
    units = last.shape[1]
    small = (features.shape[0] + mid.shape[0], units)
    dma, vmem = pltpu.SemaphoreType.DMA, pl.BlockSpec(memory_space=pltpu.VMEM)
    half, wide = jnp.bfloat16, jnp.float32
    forward, inverse = fourier_tables(width)
    gated, cot_all, spread, back, last_all, small_all = pl.pallas_call(
        functools.partial(layer_kernel, lines, columns, parts, tokens, share, width),
        out_shape=[
            jax.ShapeDtypeStruct((rows, length), half),
            jax.ShapeDtypeStruct((cot.shape[0], length), half),
            jax.ShapeDtypeStruct(spread_shape, half),
            jax.ShapeDtypeStruct((3, cycle, rows, tokens), half),
            jax.ShapeDtypeStruct((cycle,) + last.shape, wide),
            jax.ShapeDtypeStruct(small, wide),
        ],
        in_specs=in_any(1) + [vmem] + in_any(1) + [vmem] * 13,
        out_specs=[vmem] + in_any(4) + [vmem],
        scratch_shapes=[
            pltpu.VMEM((3, rows, length), half),
            pltpu.VMEM((3, rows, length), wide),
            pltpu.VMEM((rows, length), wide),
            pltpu.VMEM((rows, length), wide),
            pltpu.VMEM((blocks * rows, 2 * width), wide),
            pltpu.VMEM((blocks * rows, 2 * width), wide),
            pltpu.VMEM((rows, length), half),
            pltpu.VMEM((3, rows, length), half),
            pltpu.VMEM(last.shape, wide),
            pltpu.VMEM(small, wide),
            pltpu.VMEM((cycle,) + small, wide),
            pltpu.VMEM(small, wide),
            pltpu.VMEM((groups,) + small, wide),
            pltpu.VMEM((lines, channels, tokens), half),
            pltpu.VMEM((lines, channels, tokens), half),
            pltpu.VMEM((lines, channels, tokens), half),
            pltpu.VMEM((cycle, rows, tokens), half),
            dma((cycle,)),
            dma((cycle,)),
            dma((lines,)),
            dma((lines,)),
            dma((lines,)),
            dma((lines,)),
            dma((cycle,)),
            dma((cycle,)),
            dma((2, columns)),
            dma((cycle,)),
            dma((count, lines)),
            dma((count, lines, most)),
            dma((count, lines, most, most)),
            dma((count, lines, most, most)),
            dma((groups if parts else 1, cycle, count)),
            dma((6,)),
            dma((3, cycle)),
            dma((3, cycle)),
            dma((groups,)),
            dma((groups,)),
        ],
        compiler_params=pltpu.CompilerParams(
            collective_id=ident, has_side_effects=True, vmem_limit_bytes=56 * 2**20
        ),
    )(streams, terms, cot, taps, skip, env, last, last.T, mid, *hidden, features, forward, inverse)
    if not parts:
        spread = lax.all_gather(lax.all_gather(gated[:share], "ctx"), "ch")
    return cot_all, spread[:, :, :share], back[:, :, :share], last_all[:, :share], small_all


def band_features(bands, length):
    phases = 2.0 * math.pi / length * (np.arange(1, bands + 1)[:, None] * np.arange(length) % length)
    return np.concatenate([np.cos(phases), np.sin(phases)]).astype(np.float32)


def fourier_tables(width):
    double = 2 * width
    row, col = np.arange(width), np.arange(double)
    phase = 2.0 * math.pi / double * (row[:, None] * row[None, :] % double)
    forward_cos = np.cos(phase)
    forward_sin = np.where(row[None, :] == 0, (1 - 2 * (row % 2))[:, None], -np.sin(phase))
    phase = 2.0 * math.pi / double * (row[:, None] * col[None, :] % double)
    inverse_cos = np.where(row == 0, 1.0, 2.0)[:, None] / double * np.cos(phase)
    inverse_sin = np.where(
        row[:, None] == 0, (1 - 2 * (col % 2))[None, :] / double, -2.0 / double * np.sin(phase)
    )
    return (
        np.concatenate([forward_cos, forward_sin], axis=1).astype(np.float32),
        np.concatenate([inverse_cos, inverse_sin], axis=0).astype(np.float32),
    )


def spectral_product(left, right, width):
    lr, li = left[..., :width], left[..., width:]
    rr, ri = right[..., :width], right[..., width:]
    edge = lax.broadcasted_iota(jnp.int32, lr.shape, lr.ndim - 1) == 0
    cross = li * ri
    real = lr * rr - jnp.where(edge, 0.0, cross)
    imag = jnp.where(edge, cross, lr * ri + li * rr)
    return jnp.concatenate([real, imag], axis=-1)


def spectral_adjoint(left, right, width):
    lr, li = left[..., :width], left[..., width:]
    rr, ri = right[..., :width], right[..., width:]
    edge = lax.broadcasted_iota(jnp.int32, lr.shape, lr.ndim - 1) == 0
    cross = li * ri
    real = lr * rr + jnp.where(edge, 0.0, cross)
    imag = jnp.where(edge, cross, lr * ri - li * rr)
    return jnp.concatenate([real, imag], axis=-1)


def total(terms):
    terms = list(terms)
    value = terms[0]
    for term in terms[1:]:
        value = value + term
    return value


def short_apply(signal, taps):
    out = taps[:, 0:1] * signal
    for lag in range(1, taps.shape[1]):
        empty = jnp.zeros((signal.shape[0], lag), signal.dtype)
        out = out + taps[:, lag : lag + 1] * jnp.concatenate([empty, signal[:, :-lag]], axis=1)
    return out


def short_adjoint(signal, taps):
    out = taps[:, 0:1] * signal
    for lag in range(1, taps.shape[1]):
        empty = jnp.zeros((signal.shape[0], lag), signal.dtype)
        out = out + taps[:, lag : lag + 1] * jnp.concatenate([signal[:, lag:], empty], axis=1)
    return out


def shards(
    streams,
    short_taps,
    filter_in,
    filter_mid,
    filter_out,
    decay_rate,
    skip_gain,
    out_weight,
    grad_out,
):
    channels, tokens = streams.shape[1:]
    cycle, groups = lax.axis_size("ctx"), lax.axis_size("ch")
    ctx = lax.axis_index("ctx")
    length = tokens * cycle
    share = channels // cycle
    spare = -share % 16

    def padded(value, axis):
        pads = [(0, 0)] * value.ndim
        pads[axis] = (0, spare)
        return jnp.pad(value, pads) if spare else value

    def mine(value, axis):
        return padded(lax.dynamic_slice_in_dim(value, ctx * share, share, axis), axis)

    pieces = padded(streams.reshape(3, cycle, share, tokens), 2)
    terms = jnp.einsum("dc,dt->ct", out_weight, grad_out, preferred_element_type=jnp.float32)
    terms = terms.astype(jnp.bfloat16).reshape(groups, channels, tokens)
    features = band_features(filter_in.shape[0] // 2, length)
    before_one = jnp.einsum("fh,fs->hs", filter_in, features, precision=precise)
    one = jnp.sin(before_one)
    before_two = jnp.einsum("gh,gs->hs", filter_mid, one, precision=precise)
    hidden = [one, jnp.cos(before_one), jnp.sin(before_two), jnp.cos(before_two)]
    rate = mine(decay_rate, 0)[:, None]
    env = jnp.exp(-rate * jnp.arange(length).astype(jnp.float32)) * jnp.sqrt(rate)

    grad_all, gated, back, last, small = layer(
        0, pieces, terms, grad_out, mine(short_taps, 1), mine(skip_gain, 0)[:, None], env,
        mine(filter_out, 1).T, filter_mid, hidden, features, share,
    )
    gated = gated.reshape(groups * channels, length)
    here = lax.dynamic_slice_in_dim(gated, ctx * tokens, tokens, 1)
    layer_out = jnp.dot(out_weight, here, preferred_element_type=jnp.float32).astype(jnp.bfloat16)
    weight_grad = jnp.einsum("dt,ct->dc", grad_all, gated, preferred_element_type=jnp.float32)
    grad_filter_out = last.reshape(channels, filter_out.shape[0]).T
    cut = filter_in.shape[0]
    return (
        layer_out, back.reshape(streams.shape), small[:cut], small[cut:], grad_filter_out, weight_grad
    )


def solution(mesh):
    return jax.shard_map(
        shards,
        mesh=mesh,
        in_specs=(
            P(None, "ch", "ctx"),
            P(None, "ch", None),
            P(),
            P(),
            P(None, "ch"),
            P("ch"),
            P("ch"),
            P("ch", None),
            P("ch", "ctx"),
        ),
        out_specs=(P("ch", "ctx"), P(None, "ch", "ctx"), P(), P(), P(None, "ch"), P("ch", None)),
        check_vma=False,
    )
```

time: 192 us -> 168 us (0.88)
  matrix products: 44.5 us -> 28.6 us
  other arithmetic: 11.8 us -> 1.79 us
  Pallas kernels: 117 us -> 127 us
  local copies, waits for them, and re-layouts: 14.7 us -> 7.67 us
    dot_general x35 -> x2, matrix products: 22.1 us -> 5.99 us  [the longest x1 3.07 us: shards(): before_two = jnp.einsum('gh,gs->hs', filter_mid, one, precision=precise)]
    pallas_call x3 -> x1, Pallas kernels: 117 us -> 127 us  [layer(): pl.pallas_call(functools.partial(layer_kernel, lines, columns, parts, tok...]
    unnamed x123 -> x12, local copies, waits for them, and re-layouts: 7.6 us -> 1.81 us
    convert_element_type x5 -> x1, other arithmetic: 5.14 us -> 0.01 us  [shards(): jnp.arange(length).astype(jnp.float32)]
    add x10 -> x0, other arithmetic: 4.93 us -> none  [the longest x1 4.11 us: short_apply(): out = out + taps[..., lag:lag + 1] * moved]
where the time goes in v1:
time: 168 us; the launch traced here: 166 us
  Pallas kernels  127 us (76%)
  matrix products  28.6 us (17%)
  local copies, waits for them, and re-layouts  7.67 us (5%)
  other arithmetic  1.79 us (1%)
    pallas_call x1, Pallas kernels, layer(): pl.pallas_call(functools.partial(layer_kernel, lines, columns, parts, tok...  127 us
    dot_general x1, matrix products, shards(): jnp.einsum('dt,ct->dc', grad_all, gated, preferred_element_type=jnp.float32)  11 us
    dot_general x1, matrix products, shards(): jnp.einsum('dc,dt->ct', out_weight, grad_out, preferred_element_type=jnp....  6.01 us
    dot_general x1, matrix products, shards(): jnp.dot(out_weight, here, preferred_element_type=jnp.float32)  5.59 us

profile of v1, /device:TPU:0, one launch (start us, length us, event | category | flops | bytes accessed | tf_op | source)
XLA Modules:
  0.0 165.7 jit_solution(13886283069517343635)
XLA Ops:
  0.6 0.0 copy-start
  0.7 0.8 dynamic-slice_negate_fusion
  1.5 1.0 exponential_multiply_fusion.env_ref
  2.4 0.8 constant_dynamic-slice_fusion.1
  3.2 0.9 copy.26.taps_ref
  4.1 0.0 copy-done
  4.1 0.1 fusion.19
  4.2 0.7 copy.24.last_ref
  4.9 0.8 dynamic_slice.16
  5.7 0.8 copy.23.skip_ref
  6.5 0.7 constant_dynamic-slice_fusion.last_flat_ref
  7.2 2.9 %cosine_bitcast_fusion = (f32[64,1024]{1,0:T(8,128)}, f32[1024,64]{0,1:T(8,128)S(1)}) fusion(f32[32,1024]{1,0:T(8,128)} %constant.21.clone.features_ref, f32[32,64]{1,0:T(8,128)} %param.15), kind=kOutput, calls=%fused_computation.6 | convolution fusion | flops 25165824 | bytes 663552 | tf_op jit(solution)/shard_map/fh,fs->hs/dot_general | solution.py:536
  10.1 0.0 copy-start.1
  10.1 3.1 %cosine_bitcast_fusion.1 = (f32[64,1024]{1,0:T(8,128)}, f32[64,1024]{1,0:T(8,128)}) fusion(f32[1024,64]{0,1:T(8,128)S(1)} %get-tuple-element.19, f32[64,64]{1,0:T(8,128)} %mid_ref.1), kind=kOutput, calls=%fused_computation.7 | convolution fusion | flops 50331648 | bytes 802816 | tf_op jit(solution)/shard_map/gh,gs->hs/dot_general | solution.py:538
  13.1 6.0 %convolution_convert_fusion = bf16[4608,256]{1,0:T(8,128)(2,1)} fusion(bf16[576,4608]{1,0:T(8,128)(2,1)} %param.20, bf16[576,256]{1,0:T(8,128)(2,1)} %cot_ref.1), kind=kOutput, calls=%fused_computation | convolution fusion | flops 1360134144 | bytes 7962624 | tf_op jit(solution)/shard_map/dc,dt->ct/dot_general | solution.py:533
  19.2 0.0 copy-done.1
  19.2 127.0 %shard_map.172 = (bf16[144,1024]{1,0:T(8,128)(2,1)}, bf16[576,1024]{1,0:T(8,128)(2,1)}, bf16[8,4,144,1024]{3,2,1,0:T(8,128)(2,1)}, bf16[3,4,144,256]{3,2,1,0:T(8...) custom-call(bf16[3,4,144,256]{3,2,1,0:T(8,128)(2,1)} %bitcast.30, bf16[8,576,256]{2,1,0:T(8,128)(2,1)} %bitcast.28, ...), custom_call_target="tpu_custom_call" | custom-call | tf_op jit(solution)/shard_map/pallas_call | solution.py:380
  146.2 11.0 %fusion.9 = f32[576,4608]{1,0:T(8,128)} fusion(bf16[576,1024]{1,0:T(8,128)(2,1)} %get-tuple-element.15, bf16[4608,1024]{1,0:T(8,128)(2,1)} %bitcast.34), kind=kOutput, calls=%fused_computation.15 | convolution fusion | flops 5435817984 | bytes 21233664 | tf_op jit(solution)/shard_map/dt,ct->dc/dot_general | solution.py:550
  157.2 0.0 copy-start.3
  157.2 0.0 copy-start.4
  157.2 0.0 copy-start.2
  157.2 5.6 %fusion.5 = bf16[576,256]{1,0:T(8,128)(2,1)} fusion(bf16[576,4608]{1,0:T(8,128)(2,1)} %param.20, bf16[4608,1024]{1,0:T(8,128)(2,1)} %bitcast.35, s32[]{:T(128)S(6)} %select_n.10), kind=kOutput, calls=%fused_computation.4 | convolution fusion | flops 1359101952 | bytes 7962628 | tf_op jit(solution)/shard_map/dot_general | solution.py:549
  162.8 0.0 copy-done.3
  162.8 0.8 copy.25
  163.6 0.0 copy-done.4
  163.6 0.6 slice.7
  164.2 0.6 slice.6
  164.8 0.0 copy-done.2
  164.8 0.9 copy.28
  (1 shorter events, 0.0 us)
Async XLA Ops:
  0.6 3.5 %copy-start = (f32[64,576]{1,0:T(8,128)S(1)}, f32[64,576]{1,0:T(8,128)}, u32[]{:S(2)}) copy-start(f32[64,576]{1,0:T(8,128)} %param.17) | copy-start | bytes 442372
  10.1 9.1 %copy-start.1 = (f32[1024,64]{0,1:T(8,128)}, f32[1024,64]{0,1:T(8,128)S(1)}, u32[]{:S(2)}) copy-start(f32[1024,64]{0,1:T(8,128)S(1)} %get-tuple-element.19) | copy-start | bytes 786436
  157.2 5.6 %copy-start.3 = (f32[4,144,64]{2,1,0:T(8,128)S(1)}, f32[4,144,64]{2,1,0:T(8,128)}, u32[]{:S(2)}) copy-start(f32[4,144,64]{2,1,0:T(8,128)} %get-tuple-element.14) | copy-start | bytes 442372
  157.2 6.4 %copy-start.4 = (f32[96,64]{1,0:T(8,128)S(1)}, f32[96,64]{1,0:T(8,128)}, u32[]{:S(2)}) copy-start(f32[96,64]{1,0:T(8,128)} %get-tuple-element.13) | copy-start | bytes 73732
  157.2 7.6 %copy-start.2 = (bf16[3,4,144,256]{3,2,1,0:T(8,128)(2,1)S(1)}, bf16[3,4,144,256]{3,2,1,0:T(8,128)(2,1)}, u32[]{:S(2)}) copy-start(bf16[3,4,144,256]{3,2,1,0:T(8,128)(2,1)} %get-tuple-element.12) | copy-start | bytes 2654212
